TPU v7x, 256 devices: a whole 4x4x8 slice. The times are simulated.
256 devices in a mesh: ctx: 16 (over x, y), tp: 8 (over z), dp: 2 (over core).
Axes of the slice: x: 4, y: 4, z: 8, core: 2. Of those that a mesh axis runs over, the one named last changes fastest.
Arguments:
- projected: bfloat16 [3, 8192, 4096], P(None, ('dp', 'ctx'), 'tp'), parts along dimension 1, may hold values from -6 to 6
- short_taps: float32 [3, 7, 4096], P(None, None, 'tp'), may hold values from -2 to 2
- long_filter: float32 [4096, 4096], P('ctx', 'tp'), may hold values from -2 to 2, as said below
- skip_gain: float32 [4096], P('tp'), may hold values from -1 to 1
- w_out: bfloat16 [4096, 4096], P('tp'), may hold values from -0.125 to 0.125
Outputs:
- hyena_out: bfloat16 [8192, 4096], P(('dp', 'ctx'), 'tp'), parts along dimension 0
There are 2 independent parts, one for each index of `dp`. A program takes and returns all parts, laid end to end along the dimension named above; an argument that names none is the same for every part. Nothing has to cross between parts.
Inputs may be any that keep to these rules, and one draw needn't show every extreme that they name: `long_filter`: taps of each channel's causal filter.
All inputs are finite; a program needn't handle non-finite values.
Results may differ from a plain program's by a relative error of at most 0.014.
Values may be sent and summed in bfloat16 or wider, within the bound.
No kernel may reach another device: no remote copies, remote signals or barrier semaphores. Data moves between devices by JAX's collectives and lax.ppermute only.
A program may use at most 64 MiB of HBM per device.

v0:
```python
import math

import jax
import jax.numpy as jnp
import numpy as np
from jax import lax
from jax.experimental import pallas as pl
from jax.experimental.pallas import tpu as pltpu
from jax.sharding import PartitionSpec as P

TAPS = 7
BF16 = jnp.bfloat16
F32 = jnp.float32
VMEM_LIMIT = 50 * 1024 * 1024


def split_bf16(values):
    high = values.astype(BF16)
    return high, (values - high.astype(F32)).astype(BF16)


def lane_dft(width):
    turns = np.outer(np.arange(width), np.arange(width)) % width
    angle = 2.0 * np.pi * turns / width
    cos, sin = np.cos(angle), np.sin(angle)
    forward = np.block([[cos, -sin], [sin, cos]]).astype(np.float32)
    high = forward.astype(jnp.bfloat16)
    low = (forward - high.astype(np.float32)).astype(jnp.bfloat16)
    return np.stack([high, low]), np.stack([high.T.copy(), low.T.copy()])


def twiddles(blocks, width):
    angle = 2.0 * np.pi * np.outer(np.arange(blocks) + 0.5, np.arange(width)) / (2 * blocks * width)
    return np.stack([np.cos(angle), -np.sin(angle)]).astype(np.float32)[:, :, None, :]


def block_angle(s, k, blocks):
    return math.pi * ((s * (2 * k + 1)) % (4 * blocks)) / (2 * blocks)


def prep_kernel(projected_ref, filter_ref, out_ref):
    blocks, _, rows = out_ref.shape
    group = filter_ref.shape[1] // blocks
    for part in range(4):
        source = projected_ref[part] if part < 3 else filter_ref[...].astype(BF16)
        turned = source.T
        out_ref[:, part * group : (part + 1) * group, :] = turned.reshape(blocks, group, rows)


def over_blocks(values, k, blocks):
    even_c = even_s = odd_c = odd_s = None
    for s, value in enumerate(values):
        c, t = math.cos(block_angle(s, k, blocks)), math.sin(block_angle(s, k, blocks))
        if s == 0:
            even_c = value
            continue
        term_c, term_s = value * c, value * t
        if s % 2 == 0:
            even_c = even_c + term_c
            even_s = term_s if even_s is None else even_s + term_s
        else:
            odd_c = term_c if odd_c is None else odd_c + term_c
            odd_s = term_s if odd_s is None else odd_s + term_s
    return (even_c + odd_c, -(even_s + odd_s)), (even_c - odd_c, even_s - odd_s)


def store_split(ref_high, ref_low, rows, cols, value):
    high, low = split_bf16(value)
    ref_high[rows, cols] = high
    ref_low[rows, cols] = low


def dot3(high, low, table_ref):
    def dot(a, b):
        return jnp.dot(a, b, preferred_element_type=F32)

    return dot(high, table_ref[0]) + dot(low, table_ref[0]) + dot(high, table_ref[1])


def conv_kernel(recv_ref, taps_ref, fwd_ref, inv_ref, tw_ref, out_ref, query, gated, high, low, spec_h, spec_u):
    blocks, quad, width = recv_ref.shape
    group = quad // 4
    lane = lax.broadcasted_iota(jnp.int32, (group, width), 1)

    def tap(part, j):
        column = part * TAPS + j
        return taps_ref[:, column : column + 1]

    def shifted(now, before, amount):
        return jnp.where(lane < amount, pltpu.roll(before, amount, 1), pltpu.roll(now, amount, 1))

    zeros = jnp.zeros((group, width), F32)
    state = [[zeros] * 4 for _ in range(3)]
    for s in range(blocks):
        results = []
        for part in range(3):
            now = recv_ref[s, part * group : (part + 1) * group, :].astype(F32)
            one = shifted(now, state[part][0], 1)
            pair6 = tap(part, 6) * now
            pair4 = tap(part, 4) * now + tap(part, 5) * one + shifted(pair6, state[part][1], 2)
            pair2 = tap(part, 2) * now + tap(part, 3) * one + shifted(pair4, state[part][2], 2)
            pair0 = tap(part, 0) * now + tap(part, 1) * one + shifted(pair2, state[part][3], 2)
            state[part] = [now, pair6, pair4, pair2]
            results.append(pair0)
        query[s] = results[0]
        gated[s] = results[1] * results[2]

    def forward(load, spec):
        for c0 in range(0, group, 16):
            for l0 in range(0, width, 128):
                values = [load(s, slice(c0, c0 + 16), slice(l0, l0 + 128)) for s in range(blocks)]
                for k in range(blocks // 2):
                    for kk, (re, im) in zip((k, blocks - 1 - k), over_blocks(values, k, blocks)):
                        tr = tw_ref[0, kk, :, l0 : l0 + 128]
                        ti = tw_ref[1, kk, :, l0 : l0 + 128]
                        rows = slice(kk * group + c0, kk * group + c0 + 16)
                        store_split(high, low, rows, slice(l0, l0 + 128), re * tr - im * ti)
                        store_split(high, low, rows, slice(width + l0, width + l0 + 128), re * ti + im * tr)
        spec[...] = dot3(high[...], low[...], fwd_ref)

    forward(lambda s, c, p: recv_ref[s, 3 * group + c.start : 3 * group + c.stop, p].astype(F32), spec_h)
    forward(lambda s, c, p: gated[s, c, p], spec_u)

    hr, hi = spec_h[:, :width], spec_h[:, width:]
    ur, ui = spec_u[:, :width], spec_u[:, width:]
    store_split(high, low, slice(None), slice(0, width), hr * ur - hi * ui)
    store_split(high, low, slice(None), slice(width, 2 * width), hr * ui + hi * ur)
    spec_h[...] = dot3(high[...], low[...], inv_ref)

    scale = 1.0 / (blocks * width)
    for c0 in range(0, group, 16):
        for l0 in range(0, width, 128):
            reals, imags = [], []
            for k in range(blocks):
                rows = slice(k * group + c0, k * group + c0 + 16)
                tr = tw_ref[0, k, :, l0 : l0 + 128] * scale
                ti = tw_ref[1, k, :, l0 : l0 + 128] * scale
                re = spec_h[rows, l0 : l0 + 128]
                im = spec_h[rows, width + l0 : width + l0 + 128]
                reals.append(re * tr + im * ti)
                imags.append(im * tr - re * ti)
            half = blocks // 2
            sum_re = [reals[k] + reals[blocks - 1 - k] for k in range(half)]
            dif_re = [reals[k] - reals[blocks - 1 - k] for k in range(half)]
            sum_im = [imags[k] + imags[blocks - 1 - k] for k in range(half)]
            dif_im = [imags[k] - imags[blocks - 1 - k] for k in range(half)]
            skip = taps_ref[c0 : c0 + 16, 3 * TAPS : 3 * TAPS + 1]
            for s in range(blocks):
                res, ims = (sum_re, dif_im) if s % 2 == 0 else (dif_re, sum_im)
                total = None
                for k in range(half):
                    angle = block_angle(s, k, blocks)
                    if s == 0:
                        term = res[k]
                    else:
                        term = res[k] * math.cos(angle) - ims[k] * math.sin(angle)
                    total = term if total is None else total + term
                at = (s, slice(c0, c0 + 16), slice(l0, l0 + 128))
                mixed = (query[at] * (total + skip * gated[at])).astype(BF16)
                out_ref[(0, *at)] = mixed
                out_ref[(1, *at)] = mixed


def project_kernel(place_ref, mixed_ref, own_ref, other_ref, out_ref):
    mine = place_ref[0]
    depth = own_ref.shape[0]
    rows = mixed_ref.shape[-1]

    def dot(part, table):
        return lax.dot_general(part, table, (((0,), (0,)), ((), ())), preferred_element_type=F32)

    first = mixed_ref[mine].reshape(depth, rows)
    second = mixed_ref[1 - mine].reshape(depth, rows)
    total = dot(first, own_ref[...]) + dot(second, other_ref[...])
    out_ref[0] = total.astype(BF16)


def local(projected, short_taps, long_filter, skip_gain, w_out):
    ctx, tp, dp = lax.axis_size("ctx"), lax.axis_size("tp"), lax.axis_size("dp")
    rows, width = projected.shape[1:]
    group = width // ctx
    me_ctx, me_tp, me_dp = lax.axis_index("ctx"), lax.axis_index("tp"), lax.axis_index("dp")

    def partner(z, d):
        first = d + (z - d) % tp // 2 * 2
        return (first + (1 - (z - d) % tp % 2)) % tp

    pair_route = [(z * dp + d, partner(z, d) * dp + d) for z in range(tp) for d in range(dp)]
    pair_groups = [
        [(c * tp + (first + d + b) % tp) * dp + d for b in range(2) for c in range(ctx)]
        for d in range(dp)
        for first in range(0, tp, 2)
    ]
    parity_groups = [list(range(odd, tp, 2)) for odd in range(2)]
    chunks = tp // 2
    parity = me_tp % 2
    place = (me_tp - me_dp) % tp % 2

    w_view = w_out.reshape(width, chunks, 2, width)
    w_send = lax.dynamic_index_in_dim(w_view, 1 - parity, 2, keepdims=False).reshape(width, chunks * width)
    w_other = lax.ppermute(w_send, ("tp", "dp"), pair_route)

    send = pl.pallas_call(
        prep_kernel,
        out_shape=jax.ShapeDtypeStruct((ctx, 4 * group, rows), BF16),
        compiler_params=pltpu.CompilerParams(vmem_limit_bytes=VMEM_LIMIT),
        name="prep",
    )(projected, long_filter)
    recv = lax.all_to_all(send, "ctx", 0, 0, tiled=True)

    table = jnp.concatenate([short_taps.reshape(3 * TAPS, width), skip_gain[None, :]], axis=0)
    table = lax.dynamic_slice_in_dim(table, me_ctx * group, group, axis=1).T
    fwd, inv = lane_dft(rows)
    mixed = pl.pallas_call(
        conv_kernel,
        out_shape=jax.ShapeDtypeStruct((2, ctx, group, rows), BF16),
        scratch_shapes=[
            pltpu.VMEM((ctx, group, rows), F32),
            pltpu.VMEM((ctx, group, rows), F32),
            pltpu.VMEM((ctx * group, 2 * rows), BF16),
            pltpu.VMEM((ctx * group, 2 * rows), BF16),
            pltpu.VMEM((ctx * group, 2 * rows), F32),
            pltpu.VMEM((ctx * group, 2 * rows), F32),
        ],
        compiler_params=pltpu.CompilerParams(vmem_limit_bytes=VMEM_LIMIT),
        name="conv",
    )(recv, table, jnp.asarray(fwd), jnp.asarray(inv), jnp.asarray(twiddles(ctx, rows)))
    mixed = lax.all_to_all(
        mixed.reshape(2 * ctx, group, rows), ("ctx", "tp", "dp"), 0, 0, tiled=True, axis_index_groups=pair_groups
    ).reshape(2, ctx, group, rows)

    partial = pl.pallas_call(
        project_kernel,
        grid_spec=pltpu.PrefetchScalarGridSpec(
            num_scalar_prefetch=1,
            grid=(chunks,),
            in_specs=[
                pl.BlockSpec((2, ctx, group, rows), lambda i, p: (0, 0, 0, 0)),
                pl.BlockSpec((width, width), lambda i, p: (0, 2 * i + p[1])),
                pl.BlockSpec((width, width), lambda i, p: (0, i)),
            ],
            out_specs=pl.BlockSpec((1, rows, width), lambda i, p: (i, 0, 0)),
        ),
        out_shape=jax.ShapeDtypeStruct((chunks, rows, width), BF16),
        compiler_params=pltpu.CompilerParams(vmem_limit_bytes=VMEM_LIMIT),
        name="project",
    )(jnp.stack([place, parity]).astype(jnp.int32), mixed, w_out, w_other)
    gathered = lax.all_to_all(partial, "tp", 0, 0, tiled=True, axis_index_groups=parity_groups)
    return jnp.sum(gathered.astype(F32), axis=0).astype(BF16)


def solution(mesh):
    in_specs = (
        P(None, ("dp", "ctx"), "tp"),
        P(None, None, "tp"),
        P("ctx", "tp"),
        P("tp"),
        P("tp", None),
    )
    out_specs = P(("dp", "ctx"), "tp")
    return jax.shard_map(local, mesh=mesh, in_specs=in_specs, out_specs=out_specs, check_vma=False)
```

profile of v0, /device:TPU:1, one launch (start us, length us, event | category | flops | bytes accessed | tf_op | source)
XLA Modules:
  0.0 120.5 jit_solution(1034620003702082656)
XLA Ops:
  0.0 7.8 %reshape.19 = bf16[512,4,2,512]{3,2,1,0:T(2,128)(2,1)} reshape(bf16[512,4096]{1,0:T(8,128)(2,1)} %own_ref.1) | data formatting | bytes 8388608 | tf_op jit(solution)/shard_map/reshape | solution.py:199
  7.8 14.3 %dynamic-slice_reduce_fusion = bf16[512,4,512]{2,1,0:T(4,128)(2,1)S(1)} fusion(bf16[512,4,2,512]{3,2,1,0:T(2,128)(2,1)} %reshape.19, s32[]{:T(128)S(6)} %select_n.26), kind=kLoop, calls=%fused_computation | loop fusion | bytes 4194308 | tf_op jit(solution)/shard_map/jit(dynamic_index_in_dim)/dynamic_slice | solution.py:200
  22.1 0.0 copy-start.5
  22.1 0.0 copy-start.6
  22.1 0.0 copy-start.4
  22.1 2.0 %copy.18 = bf16[64,8,4,512]{3,1,2,0:T(8,128)(2,1)} copy(bf16[64,8,4,512]{3,2,1,0:T(4,128)(2,1)S(1)} %bitcast.10) | data formatting | bytes 4194304
  24.1 6.4 %collective-permute-start = (bf16[512,2048]{1,0:T(8,128)(2,1)}, bf16[512,2048]{1,0:T(8,128)(2,1)S(1)}, u32[]{:S(2)}, u32[]{:S(2)}) collective-permute-start(bf16[512,2048]{1,0:T(8,128)(2,1)} %bitcast.7), channel_id=1, source_target_pairs={{0,2},{1,15},{2,0},{3,5},{4,6},{5,3},{6,4},{7,9},{8,10},{9,7},{10,... | collective-permute-start | bytes 6291464 | tf_op jit(solution)/shard_map/ppermute | solution.py:201
  30.5 0.0 copy-done.2
  30.5 1.3 %prep.1 = bf16[16,128,256]{2,1,0:T(8,128)(2,1)} custom-call(bf16[3,256,512]{2,1,0:T(8,128)(2,1)S(1)} %copy-done.2, f32[256,512]{1,0:T(8,128)S(1)} %copy-done.3), custom_call_target="tpu_custom_call" | custom-call | tf_op jit(solution)/shard_map/prep/pallas_call | solution.py:203
  31.9 6.8 %all-to-all-start = ((bf16[16,128,256]{2,1,0:T(8,128)(2,1)}), bf16[16,128,256]{2,1,0:T(8,128)(2,1)S(1)}, u32[]{:S(2)}, u32[]{:S(2)}) async-start(bf16[16,128,256]{2,1,0:T(8,128)(2,1)} %prep.1), calls=%async_computation | async-start | bytes 2097152 | tf_op jit(solution)/shard_map/all_to_all | solution.py:209
  38.7 0.1 fusion
  38.8 0.1 copy.16
  38.8 15.0 %all-to-all-done.recv_ref = bf16[16,128,256]{2,1,0:T(8,128)(2,1)S(1)} async-done(((bf16[16,128,256]{2,1,0:T(8,128)(2,1)}), bf16[16,128,256]{2,1,0:T(8,128)(2,1)S(1)}, u32[]{:S(2)}, u32[]{:S(2)}) %all-to-all-start) | async-done | bytes 1048608 | tf_op jit(solution)/shard_map/all_to_all | solution.py:209
  53.8 0.0 copy-done.4
  53.8 1.2 %copy-done = bf16[2,512,512]{2,1,0:T(8,128)(2,1)S(1)} copy-done((bf16[2,512,512]{2,1,0:T(8,128)(2,1)S(1)}, bf16[2,512,512]{2,1,0:T(8,128)(2,1)}, u32[]{:S(2)}) %copy-start) | copy-done | bytes 1048600
  55.1 1.2 %copy-done.1 = bf16[2,512,512]{2,1,0:T(8,128)(2,1)S(1)} copy-done((bf16[2,512,512]{2,1,0:T(8,128)(2,1)S(1)}, bf16[2,512,512]{2,1,0:T(8,128)(2,1)}, u32[]{:S(2)}) %copy-start.1) | copy-done | bytes 1048600
  56.3 11.7 %conv.1 = bf16[2,16,32,256]{3,2,1,0:T(8,128)(2,1)} custom-call(bf16[16,128,256]{2,1,0:T(8,128)(2,1)S(1)} %all-to-all-done.recv_ref, f32[32,22]{1,0:T(8,128)S(1)} %bitcast.9, bf16[2,512,512]{2,1,0:T(8,128)(2,1)S(1)} %copy-done, bf16[2,512,512]{2,1,0:T(8,128)(2,1)S(1)} %copy-done.1, f32[2,16,1,256]{3,2,1,0:T(1,128)S(1)} %copy-done.4), custom_call_target="tpu_custom_call" | custom-call | tf_op jit(solution)/shard_map/conv/pallas_call | solution.py:214
  68.0 5.6 %all-to-all-start.1 = ((bf16[32,32,256]{2,1,0:T(8,128)(2,1)}), bf16[32,32,256]{2,1,0:T(8,128)(2,1)S(1)}, u32[]{:S(2)}, u32[]{:S(2)}) async-start(bf16[32,32,256]{2,1,0:T(8,128)(2,1)} %bitcast.4), calls=%async_computation.1 | async-start | bytes 1048576 | tf_op jit(solution)/shard_map/all_to_all | solution.py:228
  73.6 0.1 pad_add_fusion.place_ref
  73.7 11.1 %all-to-all-done.1 = bf16[32,32,256]{2,1,0:T(8,128)(2,1)S(1)} async-done(((bf16[32,32,256]{2,1,0:T(8,128)(2,1)}), bf16[32,32,256]{2,1,0:T(8,128)(2,1)S(1)}, u32[]{:S(2)}, u32[]{:S(2)}) %all-to-all-start.1) | async-done | bytes 524320 | tf_op jit(solution)/shard_map/all_to_all | solution.py:228
  84.8 0.0 collective-permute-done.other_ref
  84.8 4.2 %project.1 = bf16[4,256,512]{2,1,0:T(8,128)(2,1)S(1)} custom-call(s32[2]{0:T(128)S(1)} %pad_add_fusion.place_ref, bf16[2,16,32,256]{3,2,1,0:T(8,128)(2,1)S(1)} %bitcast.8, bf16[512,4096]{1,0:T(8,128)(2,1)} %own_ref.1, bf16[512,2048]{1,0:T(8,128)(2,1)S(1)} %collective-permute-done.other_ref), custom_call_target="tpu_custom_call" | custom-call | tf_op jit(solution)/shard_map/project/pallas_call | solution.py:232
  89.0 30.7 %all_to_all.15 = bf16[4,256,512]{2,1,0:T(8,128)(2,1)S(1)} all-to-all(bf16[4,256,512]{2,1,0:T(8,128)(2,1)S(1)} %project.1), channel_id=1, replica_groups={{0,4,8,12},{2,6,10,14},{1,5,9,13},{3,7,11,15},{16,20,24,28},{18,22,26,3..., dimensions={0} | all-to-all | bytes 2097152 | tf_op jit(solution)/shard_map/all_to_all | solution.py:248
  119.6 0.9 reduce_sum.12
  (8 shorter events, 0.0 us)
Async XLA Ops:
  7.8 22.7 %copy-start.2 = (bf16[3,256,512]{2,1,0:T(8,128)(2,1)S(1)}, bf16[3,256,512]{2,1,0:T(8,128)(2,1)}, u32[]{:S(2)}) copy-start(bf16[3,256,512]{2,1,0:T(8,128)(2,1)} %projected_ref.1) | copy-start | bytes 2359300
  7.8 22.7 %copy-start.3 = (f32[256,512]{1,0:T(8,128)S(1)}, f32[256,512]{1,0:T(8,128)}, u32[]{:S(2)}) copy-start(f32[256,512]{1,0:T(8,128)} %filter_ref.1) | copy-start | bytes 1572868
  22.1 16.5 %copy-start.5 = (f32[3,7,512]{2,1,0:T(8,128)S(1)}, f32[3,7,512]{2,1,0:T(8,128)}, u32[]{:S(2)}) copy-start(f32[3,7,512]{2,1,0:T(8,128)} %param.9) | copy-start | bytes 129028
  22.1 16.6 %copy-start.6 = (f32[512]{0:T(512)S(1)}, f32[512]{0:T(512)}, u32[]{:S(2)}) copy-start(f32[512]{0:T(512)} %param.11) | copy-start | bytes 6148
  22.1 31.7 %copy-start.4 = (f32[2,16,1,256]{3,2,1,0:T(1,128)S(1)}, f32[2,16,1,256]{3,2,1,0:T(1,128)}, u32[]{:S(2)}) copy-start(f32[2,16,1,256]{3,2,1,0:T(1,128)} %constant.63.clone.tw_ref) | copy-start | bytes 98308
  24.1 60.7 %collective-permute-start = (bf16[512,2048]{1,0:T(8,128)(2,1)}, bf16[512,2048]{1,0:T(8,128)(2,1)S(1)}, u32[]{:S(2)}, u32[]{:S(2)}) collective-permute-start(bf16[512,2048]{1,0:T(8,128)(2,1)} %bitcast.7), channel_id=1, source_target_pairs={{0,2},{1,15},{2,0},{3,5},{4,6},{5,3},{6,4},{7,9},{8,10},{9,7},{10,... | collective-permute-start | bytes 6291464 | tf_op jit(solution)/shard_map/ppermute | solution.py:201
  31.9 22.0 %all-to-all-start = ((bf16[16,128,256]{2,1,0:T(8,128)(2,1)}), bf16[16,128,256]{2,1,0:T(8,128)(2,1)S(1)}, u32[]{:S(2)}, u32[]{:S(2)}) async-start(bf16[16,128,256]{2,1,0:T(8,128)(2,1)} %prep.1), calls=%async_computation | async-start | bytes 2097152 | tf_op jit(solution)/shard_map/all_to_all | solution.py:209
  53.8 1.2 %copy-start = (bf16[2,512,512]{2,1,0:T(8,128)(2,1)S(1)}, bf16[2,512,512]{2,1,0:T(8,128)(2,1)}, u32[]{:S(2)}) copy-start(bf16[2,512,512]{2,1,0:T(8,128)(2,1)} %constant.61.clone.fwd_ref) | copy-start | bytes 3145732
  55.1 1.2 %copy-start.1 = (bf16[2,512,512]{2,1,0:T(8,128)(2,1)S(1)}, bf16[2,512,512]{2,1,0:T(8,128)(2,1)}, u32[]{:S(2)}) copy-start(bf16[2,512,512]{2,1,0:T(8,128)(2,1)} %constant.62.clone.inv_ref) | copy-start | bytes 3145732
  68.0 16.8 %all-to-all-start.1 = ((bf16[32,32,256]{2,1,0:T(8,128)(2,1)}), bf16[32,32,256]{2,1,0:T(8,128)(2,1)S(1)}, u32[]{:S(2)}, u32[]{:S(2)}) async-start(bf16[32,32,256]{2,1,0:T(8,128)(2,1)} %bitcast.4), calls=%async_computation.1 | async-start | bytes 1048576 | tf_op jit(solution)/shard_map/all_to_all | solution.py:228
where the time goes:
time: 121 us
  blocking collectives  30.7 us (25%)
  local copies, waits for them, and re-layouts  26.6 us (22%)
  waiting for transfers between devices  26.1 us (22%)
  starting transfers between devices  18.8 us (16%)
  Pallas kernels  17.2 us (14%)
    all_to_all x1, blocking collectives, local(): lax.all_to_all(partial, 'tp', 0, 0, tiled=True, axis_index_groups=parity_...  30.7 us
    all_to_all x1, waiting for transfers between devices, local(): recv = lax.all_to_all(send, 'ctx', 0, 0, tiled=True)  15 us
    dynamic_slice x1, local copies, waits for them, and re-layouts, local(): lax.dynamic_index_in_dim(w_view, 1 - parity, 2, keepdims=False)  14.3 us
    pallas_call x1, Pallas kernels, local(): pl.pallas_call(conv_kernel, out_shape=jax.ShapeDtypeStruct((2, ctx, group...  11.7 us
    all_to_all x1, waiting for transfers between devices, local(): lax.all_to_all(mixed.reshape(2 * ctx, group, rows), ('ctx', 'tp', 'dp'),...  11.1 us
    reshape x1, local copies, waits for them, and re-layouts, local(): w_view = w_out.reshape(width, chunks, 2, width)  7.79 us
    all_to_all x1, starting transfers between devices, local(): recv = lax.all_to_all(send, 'ctx', 0, 0, tiled=True)  6.76 us
    ppermute x1, starting transfers between devices, local(): w_other = lax.ppermute(w_send, ('tp', 'dp'), pair_route)  6.41 us
  transfers between devices with their start and end apart: 3, of which 2 were waited for; matrix products, arithmetic and copies ran while one was open for 0% of the time, Pallas kernels for 11%

commit v1 on v0

--- a/solution.py
+++ b/solution.py
@@ -38,13 +38,25 @@
     return math.pi * ((s * (2 * k + 1)) % (4 * blocks)) / (2 * blocks)
 
 
-def prep_kernel(projected_ref, filter_ref, out_ref):
+def prep_kernel(parity_ref, projected_ref, filter_ref, w_ref, out_ref, w_send_ref, sems):
     blocks, _, rows = out_ref.shape
-    group = filter_ref.shape[1] // blocks
+    width = filter_ref.shape[1]
+    group = width // blocks
+    copies = []
+    for i in range(w_send_ref.shape[1] // width):
+        start = pl.multiple_of((2 * i + 1 - parity_ref[0]) * width, width)
+        copies.append(
+            pltpu.make_async_copy(
+                w_ref.at[:, pl.ds(start, width)], w_send_ref.at[:, i * width : (i + 1) * width], sems.at[i]
+            )
+        )
+        copies[-1].start()
     for part in range(4):
         source = projected_ref[part] if part < 3 else filter_ref[...].astype(BF16)
         turned = source.T
         out_ref[:, part * group : (part + 1) * group, :] = turned.reshape(blocks, group, rows)
+    for copy in copies:
+        copy.wait()
 
 
 def over_blocks(values, k, blocks):
@@ -77,8 +89,14 @@
     return dot(high, table_ref[0]) + dot(low, table_ref[0]) + dot(high, table_ref[1])
 
 
-def conv_kernel(recv_ref, taps_ref, fwd_ref, inv_ref, tw_ref, out_ref, query, gated, high, low, spec_h, spec_u):
+def conv_kernel(
+    recv_ref, taps_ref, fwd_hbm, inv_hbm, tw_ref, out_ref, query, gated, high, low, spec_h, spec_u, fwd_ref, inv_ref, sems
+):
     blocks, quad, width = recv_ref.shape
+    fwd_copy = pltpu.make_async_copy(fwd_hbm, fwd_ref, sems.at[0])
+    inv_copy = pltpu.make_async_copy(inv_hbm, inv_ref, sems.at[1])
+    fwd_copy.start()
+    inv_copy.start()
     group = quad // 4
     lane = lax.broadcasted_iota(jnp.int32, (group, width), 1)
 
@@ -105,7 +123,7 @@
         query[s] = results[0]
         gated[s] = results[1] * results[2]
 
-    def forward(load, spec):
+    def forward(load, _):
         for c0 in range(0, group, 16):
             for l0 in range(0, width, 128):
                 values = [load(s, slice(c0, c0 + 16), slice(l0, l0 + 128)) for s in range(blocks)]
@@ -116,15 +134,18 @@
                         rows = slice(kk * group + c0, kk * group + c0 + 16)
                         store_split(high, low, rows, slice(l0, l0 + 128), re * tr - im * ti)
                         store_split(high, low, rows, slice(width + l0, width + l0 + 128), re * ti + im * tr)
-        spec[...] = dot3(high[...], low[...], fwd_ref)
 
     forward(lambda s, c, p: recv_ref[s, 3 * group + c.start : 3 * group + c.stop, p].astype(F32), spec_h)
+    fwd_copy.wait()
+    spec_h[...] = dot3(high[...], low[...], fwd_ref)
     forward(lambda s, c, p: gated[s, c, p], spec_u)
+    spec_u[...] = dot3(high[...], low[...], fwd_ref)
 
     hr, hi = spec_h[:, :width], spec_h[:, width:]
     ur, ui = spec_u[:, :width], spec_u[:, width:]
     store_split(high, low, slice(None), slice(0, width), hr * ur - hi * ui)
     store_split(high, low, slice(None), slice(width, 2 * width), hr * ui + hi * ur)
+    inv_copy.wait()
     spec_h[...] = dot3(high[...], low[...], inv_ref)
 
     scale = 1.0 / (blocks * width)
@@ -161,17 +182,18 @@
                 out_ref[(1, *at)] = mixed
 
 
-def project_kernel(place_ref, mixed_ref, own_ref, other_ref, out_ref):
+def project_kernel(place_ref, mixed_ref, own_ref, other_ref, out_ref, turned):
     mine = place_ref[0]
     depth = own_ref.shape[0]
     rows = mixed_ref.shape[-1]
 
-    def dot(part, table):
-        return lax.dot_general(part, table, (((0,), (0,)), ((), ())), preferred_element_type=F32)
-
-    first = mixed_ref[mine].reshape(depth, rows)
-    second = mixed_ref[1 - mine].reshape(depth, rows)
-    total = dot(first, own_ref[...]) + dot(second, other_ref[...])
+    @pl.when(pl.program_id(0) == 0)
+    def _():
+        turned[0] = mixed_ref[mine].reshape(depth, rows).T
+        turned[1] = mixed_ref[1 - mine].reshape(depth, rows).T
+
+    total = jnp.dot(turned[0], own_ref[...], preferred_element_type=F32)
+    total += jnp.dot(turned[1], other_ref[...], preferred_element_type=F32)
     out_ref[0] = total.astype(BF16)
 
 
@@ -196,16 +218,21 @@
     parity = me_tp % 2
     place = (me_tp - me_dp) % tp % 2
 
-    w_view = w_out.reshape(width, chunks, 2, width)
-    w_send = lax.dynamic_index_in_dim(w_view, 1 - parity, 2, keepdims=False).reshape(width, chunks * width)
-    w_other = lax.ppermute(w_send, ("tp", "dp"), pair_route)
-
-    send = pl.pallas_call(
+    whole = pl.BlockSpec()
+    in_place = pl.BlockSpec(memory_space=pl.ANY)
+    send, w_send = pl.pallas_call(
         prep_kernel,
-        out_shape=jax.ShapeDtypeStruct((ctx, 4 * group, rows), BF16),
+        in_specs=[pl.BlockSpec(memory_space=pltpu.SMEM), whole, whole, in_place],
+        out_specs=[whole, in_place],
+        out_shape=[
+            jax.ShapeDtypeStruct((ctx, 4 * group, rows), BF16),
+            jax.ShapeDtypeStruct((width, chunks * width), BF16),
+        ],
+        scratch_shapes=[pltpu.SemaphoreType.DMA((chunks,))],
         compiler_params=pltpu.CompilerParams(vmem_limit_bytes=VMEM_LIMIT),
         name="prep",
-    )(projected, long_filter)
+    )(parity.astype(jnp.int32)[None], projected, long_filter, w_out)
+    w_other = lax.ppermute(w_send, ("tp", "dp"), pair_route)
     recv = lax.all_to_all(send, "ctx", 0, 0, tiled=True)
 
     table = jnp.concatenate([short_taps.reshape(3 * TAPS, width), skip_gain[None, :]], axis=0)
@@ -221,7 +248,11 @@
             pltpu.VMEM((ctx * group, 2 * rows), BF16),
             pltpu.VMEM((ctx * group, 2 * rows), F32),
             pltpu.VMEM((ctx * group, 2 * rows), F32),
+            pltpu.VMEM((2, 2 * rows, 2 * rows), BF16),
+            pltpu.VMEM((2, 2 * rows, 2 * rows), BF16),
+            pltpu.SemaphoreType.DMA((2,)),
         ],
+        in_specs=[whole, whole, in_place, in_place, whole],
         compiler_params=pltpu.CompilerParams(vmem_limit_bytes=VMEM_LIMIT),
         name="conv",
     )(recv, table, jnp.asarray(fwd), jnp.asarray(inv), jnp.asarray(twiddles(ctx, rows)))
@@ -240,6 +271,7 @@
                 pl.BlockSpec((width, width), lambda i, p: (0, i)),
             ],
             out_specs=pl.BlockSpec((1, rows, width), lambda i, p: (i, 0, 0)),
+            scratch_shapes=[pltpu.VMEM((2, rows, width), BF16)],
         ),
         out_shape=jax.ShapeDtypeStruct((chunks, rows, width), BF16),
         compiler_params=pltpu.CompilerParams(vmem_limit_bytes=VMEM_LIMIT),

time: 121 us -> 169 us (1.40)
  Pallas kernels: 17.2 us -> 85.6 us
  local copies, waits for them, and re-layouts: 26.6 us -> 5.71 us
    pallas_call x1, Pallas kernels: 1.33 us -> 64.7 us  [local(): pl.pallas_call(prep_kernel, in_specs=[pl.BlockSpec(memory_space=pltpu.SME...]
    dynamic_slice x1 -> x0, local copies, waits for them, and re-layouts: 14.3 us -> none  [local(): lax.dynamic_index_in_dim(w_view, 1 - parity, 2, keepdims=False)]
    reshape x1 -> x0, local copies, waits for them, and re-layouts: 7.79 us -> none  [local(): w_view = w_out.reshape(width, chunks, 2, width)]
    pallas_call x1, Pallas kernels: 11.7 us -> 16.7 us  [local(): pl.pallas_call(conv_kernel, out_shape=jax.ShapeDtypeStruct((2, ctx, group...]
    unnamed x16 -> x17, local copies, waits for them, and re-layouts: 4.55 us -> 5.7 us
  transfers between devices with their start and end apart: 3 -> 3, of which waited for: 2 -> 2; matrix products, arithmetic and copies ran while one was open for 0% -> 0% of each run, Pallas kernels for 11% -> 10%
where the time goes in v1:
time: 169 us; the launch traced here: 168 us
  Pallas kernels  85.6 us (51%)
  blocking collectives  30.7 us (18%)
  waiting for transfers between devices  26.1 us (15%)
  starting transfers between devices  18.8 us (11%)
  local copies, waits for them, and re-layouts  5.71 us (3%)
    pallas_call x1, Pallas kernels, local(): pl.pallas_call(prep_kernel, in_specs=[pl.BlockSpec(memory_space=pltpu.SME...  64.7 us
    all_to_all x1, blocking collectives, local(): lax.all_to_all(partial, 'tp', 0, 0, tiled=True, axis_index_groups=parity_...  30.7 us
    pallas_call x1, Pallas kernels, local(): pl.pallas_call(conv_kernel, out_shape=jax.ShapeDtypeStruct((2, ctx, group...  16.7 us
    all_to_all x1, waiting for transfers between devices, local(): recv = lax.all_to_all(send, 'ctx', 0, 0, tiled=True)  15 us
    all_to_all x1, waiting for transfers between devices, local(): lax.all_to_all(mixed.reshape(2 * ctx, group, rows), ('ctx', 'tp', 'dp'),...  11.1 us
    all_to_all x1, starting transfers between devices, local(): recv = lax.all_to_all(send, 'ctx', 0, 0, tiled=True)  6.75 us
    ppermute x1, starting transfers between devices, local(): w_other = lax.ppermute(w_send, ('tp', 'dp'), pair_route)  6.41 us
    unnamed x17, local copies, waits for them, and re-layouts  5.7 us
  transfers between devices with their start and end apart: 3, of which 2 were waited for; matrix products, arithmetic and copies ran while one was open for 0% of the time, Pallas kernels for 10%

profile of v1, /device:TPU:1, one launch (start us, length us, event | category | flops | bytes accessed | tf_op | source)
XLA Modules:
  0.0 168.1 jit_solution(8643930785504995464)
XLA Ops:
  0.0 0.0 copy-start.3
  0.0 1.1 copy-done.3
  1.1 1.0 copy-done.4
  2.2 64.7 %prep.1 = (bf16[16,128,256]{2,1,0:T(8,128)(2,1)S(1)}, bf16[512,2048]{1,0:T(8,128)(2,1)}) custom-call(s32[1]{0:T(128)} %bitcast.1.parity_ref, bf16[3,256,512]{2,1,0:T(8,128)(2,1)S(1)} %copy-done.3, f32[256,512]{1,0:T(8,128)S(1)} %copy-done.4, bf16[512,4096]{1,0:T(8,128)(2,1)} %own_ref.1), custom_call_target="tpu_custom_call" | custom-call | tf_op jit(solution)/shard_map/prep/pallas_call | solution.py:223
  66.8 0.0 copy-start.2
  66.9 1.0 copy-done.2
  67.8 6.4 %collective-permute-start = (bf16[512,2048]{1,0:T(8,128)(2,1)}, bf16[512,2048]{1,0:T(8,128)(2,1)S(1)}, u32[]{:S(2)}, u32[]{:S(2)}) collective-permute-start(bf16[512,2048]{1,0:T(8,128)(2,1)} %get-tuple-element.8), channel_id=1, source_target_pairs={{0,2},{1,15},{2,0},{3,5},{4,6},{5,3},{6,4},{7,9},{8,10},{9,7},{10,... | collective-permute-start | bytes 6291464 | tf_op jit(solution)/shard_map/ppermute | solution.py:235
  74.2 6.8 %all-to-all-start = ((bf16[16,128,256]{2,1,0:T(8,128)(2,1)}), bf16[16,128,256]{2,1,0:T(8,128)(2,1)S(1)}, u32[]{:S(2)}, u32[]{:S(2)}) async-start(bf16[16,128,256]{2,1,0:T(8,128)(2,1)} %copy-done.2), calls=%async_computation | async-start | bytes 2097152 | tf_op jit(solution)/shard_map/all_to_all | solution.py:236
  81.0 0.0 copy-done.6
  81.0 0.0 copy-done.7
  81.1 0.1 fusion
  81.1 0.1 copy.13
  81.2 15.0 %all-to-all-done.recv_ref = bf16[16,128,256]{2,1,0:T(8,128)(2,1)S(1)} async-done(((bf16[16,128,256]{2,1,0:T(8,128)(2,1)}), bf16[16,128,256]{2,1,0:T(8,128)(2,1)S(1)}, u32[]{:S(2)}, u32[]{:S(2)}) %all-to-all-start) | async-done | bytes 1048608 | tf_op jit(solution)/shard_map/all_to_all | solution.py:236
  96.2 0.0 copy-done.5
  96.2 1.2 copy-done
  97.5 1.2 copy-done.1
  98.7 16.7 %conv.1 = bf16[2,16,32,256]{3,2,1,0:T(8,128)(2,1)} custom-call(bf16[16,128,256]{2,1,0:T(8,128)(2,1)S(1)} %all-to-all-done.recv_ref, f32[32,22]{1,0:T(8,128)S(1)} %bitcast.7, bf16[2,512,512]{2,1,0:T(8,128)(2,1)S(1)} %copy-done.1, bf16[2,512,512]{2,1,0:T(8,128)(2,1)S(1)} %copy-done, f32[2,16,1,256]{3,2,1,0:T(1,128)S(1)} %copy-done.5), custom_call_target="tpu_custom_call" | custom-call | tf_op jit(solution)/shard_map/conv/pallas_call | solution.py:241
  115.4 5.6 %all-to-all-start.1 = ((bf16[32,32,256]{2,1,0:T(8,128)(2,1)}), bf16[32,32,256]{2,1,0:T(8,128)(2,1)S(1)}, u32[]{:S(2)}, u32[]{:S(2)}) async-start(bf16[32,32,256]{2,1,0:T(8,128)(2,1)} %bitcast.4), calls=%async_computation.1 | async-start | bytes 1048576 | tf_op jit(solution)/shard_map/all_to_all | solution.py:259
  121.0 0.1 pad_add_fusion.place_ref
  121.1 11.1 %all-to-all-done.1 = bf16[32,32,256]{2,1,0:T(8,128)(2,1)S(1)} async-done(((bf16[32,32,256]{2,1,0:T(8,128)(2,1)}), bf16[32,32,256]{2,1,0:T(8,128)(2,1)S(1)}, u32[]{:S(2)}, u32[]{:S(2)}) %all-to-all-start.1) | async-done | bytes 524320 | tf_op jit(solution)/shard_map/all_to_all | solution.py:259
  132.2 0.0 collective-permute-done.other_ref
  132.2 4.3 %project.1 = bf16[4,256,512]{2,1,0:T(8,128)(2,1)S(1)} custom-call(s32[2]{0:T(128)S(1)} %pad_add_fusion.place_ref, bf16[2,16,32,256]{3,2,1,0:T(8,128)(2,1)S(1)} %bitcast.6, bf16[512,4096]{1,0:T(8,128)(2,1)} %own_ref.1, bf16[512,2048]{1,0:T(8,128)(2,1)S(1)} %collective-permute-done.other_ref), custom_call_target="tpu_custom_call" | custom-call | tf_op jit(solution)/shard_map/project/pallas_call | solution.py:263
  136.5 30.7 %all_to_all.15 = bf16[4,256,512]{2,1,0:T(8,128)(2,1)S(1)} all-to-all(bf16[4,256,512]{2,1,0:T(8,128)(2,1)S(1)} %project.1), channel_id=1, replica_groups={{0,4,8,12},{2,6,10,14},{1,5,9,13},{3,7,11,15},{16,20,24,28},{18,22,26,3..., dimensions={0} | all-to-all | bytes 2097152 | tf_op jit(solution)/shard_map/all_to_all | solution.py:280
  167.1 0.9 reduce_sum.12
  (7 shorter events, 0.0 us)
Async XLA Ops:
  0.0 1.1 copy-start.3
  1.1 1.0 copy-start.4
  66.8 1.0 copy-start.2
  67.8 13.2 %copy-start.6 = (f32[3,7,512]{2,1,0:T(8,128)S(1)}, f32[3,7,512]{2,1,0:T(8,128)}, u32[]{:S(2)}) copy-start(f32[3,7,512]{2,1,0:T(8,128)} %param.9) | copy-start | bytes 129028
  67.8 13.2 %copy-start.7 = (f32[512]{0:T(512)S(1)}, f32[512]{0:T(512)}, u32[]{:S(2)}) copy-start(f32[512]{0:T(512)} %param.11) | copy-start | bytes 6148
  67.8 28.4 %copy-start.5 = (f32[2,16,1,256]{3,2,1,0:T(1,128)S(1)}, f32[2,16,1,256]{3,2,1,0:T(1,128)}, u32[]{:S(2)}) copy-start(f32[2,16,1,256]{3,2,1,0:T(1,128)} %constant.56.clone.tw_ref) | copy-start | bytes 98308
  67.8 64.3 %collective-permute-start = (bf16[512,2048]{1,0:T(8,128)(2,1)}, bf16[512,2048]{1,0:T(8,128)(2,1)S(1)}, u32[]{:S(2)}, u32[]{:S(2)}) collective-permute-start(bf16[512,2048]{1,0:T(8,128)(2,1)} %get-tuple-element.8), channel_id=1, source_target_pairs={{0,2},{1,15},{2,0},{3,5},{4,6},{5,3},{6,4},{7,9},{8,10},{9,7},{10,... | collective-permute-start | bytes 6291464 | tf_op jit(solution)/shard_map/ppermute | solution.py:235
  74.2 22.0 %all-to-all-start = ((bf16[16,128,256]{2,1,0:T(8,128)(2,1)}), bf16[16,128,256]{2,1,0:T(8,128)(2,1)S(1)}, u32[]{:S(2)}, u32[]{:S(2)}) async-start(bf16[16,128,256]{2,1,0:T(8,128)(2,1)} %copy-done.2), calls=%async_computation | async-start | bytes 2097152 | tf_op jit(solution)/shard_map/all_to_all | solution.py:236
  96.2 1.2 copy-start
  97.5 1.2 copy-start.1
  115.4 16.8 %all-to-all-start.1 = ((bf16[32,32,256]{2,1,0:T(8,128)(2,1)}), bf16[32,32,256]{2,1,0:T(8,128)(2,1)S(1)}, u32[]{:S(2)}, u32[]{:S(2)}) async-start(bf16[32,32,256]{2,1,0:T(8,128)(2,1)} %bitcast.4), calls=%async_computation.1 | async-start | bytes 1048576 | tf_op jit(solution)/shard_map/all_to_all | solution.py:259
